TPU v7x, 256 devices: a whole 4x4x8 slice. The times are simulated.
256 devices in a mesh: domain: 128 (over z, x, y_lo, core), band: 2 (over y_hi).
Axes of the slice: x: 4, y: 4 (y_hi: 2, y_lo: 2; y = y_hi * 2 + y_lo), z: 8, core: 2. Of those that a mesh axis runs over, the one named last changes fastest.
Arguments:
- orbitals: float32 [64, 262144], P('band', 'domain'), may hold values from -6 to 6
- others: float32 [192, 262144], P('band', 'domain'), may hold values from -6 to 6
- potential: float32 [262144], P('domain'), may hold values from -8 to 8
- cell_scale: float32 [98304], P('domain'), may hold values from 0.5 to 2
- connectivity: int32 [64, 98304], P(None, 'domain'), may hold values from 0 to 5119, as said below
- send_up: int32 [196608], P('domain'), may hold values from 0 to 2047, as said below
- send_down: int32 [196608], P('domain'), may hold values from 0 to 2047, as said below
- stiffness: float32 [64, 64], replicated, may hold values from -0.25 to 3, as said below
- rotation: float32 [256, 256], replicated, may hold values from -0.375 to 0.375
Outputs:
- rotated: float32 [256, 262144], P('band', 'domain')
Inputs may be any that keep to these rules, and one draw needn't show every extreme that they name: `connectivity`: positions of a slab's extended node list: the first 1536 are the previous slab's shared nodes in the order of its send_up list, the next 2048 the slab's own nodes, the last 1536 the next slab's shared nodes in the order of its send_down list. The nodes of the cell numbered j within its slab lie among the 256 consecutive positions that begin at j * 4864 // 767. Within a slab, cells numbered below 288 have all nodes among the first 2560 positions and the others none among the first 1536; cells numbered 768 - 288 or more have all nodes among the last 2560 positions and the others none among the last 1536. `send_up`: for each slab in turn, 1536 distinct node numbers within that slab. `send_down`: for each slab in turn, 1536 distinct node numbers within that slab. `stiffness`: Symmetric.
All inputs are finite; a program needn't handle non-finite values.
Results may differ from a plain program's by a relative error of at most 0.0001.
Values sent between devices are 32-bit elements; how exact they have to be, the bound alone decides.
A program may use at most 64 MiB of HBM per device.

v0:
```python
import math

import jax
import jax.numpy as jnp
from jax import lax
from jax.sharding import PartitionSpec as P

WINDOW = 256


FILTER_CENTER = 64.0
FILTER_HALF = 64.0


def shifted(block, axis, distance):
    devices = range(lax.axis_size(axis))
    route = [((i - distance) % len(devices), i) for i in devices]
    return lax.ppermute(block, axis, route)


def with_halo(cells, sides, width):
    for axis, dim in sides:
        count = lax.axis_size(axis)
        head = lax.slice_in_dim(cells, 0, width, axis=dim)
        tail = lax.slice_in_dim(cells, cells.shape[dim] - width, cells.shape[dim], axis=dim)
        cells = jnp.concatenate(
            [
                lax.ppermute(tail, axis, [(i, (i + 1) % count) for i in range(count)]),
                cells,
                lax.ppermute(head, axis, [((i + 1) % count, i) for i in range(count)]),
            ],
            axis=dim,
        )
    return cells


def weighted(weights, portion):
    return jnp.einsum(
        "io,in->on",
        weights,
        portion,
        precision=lax.Precision.HIGHEST,
        preferred_element_type=jnp.float32,
    )


def cell_images(stiffness, values, scales):
    return jnp.einsum("ij,ojc->oic", stiffness, values, precision=lax.Precision.HIGHEST) * scales


def picked(vectors, selector):
    return jnp.dot(
        vectors, selector, precision=lax.Precision.HIGHEST, preferred_element_type=jnp.float32
    )


def placed(values, selector):
    return jnp.einsum(
        "or,nr->on",
        values,
        selector,
        precision=lax.Precision.HIGHEST,
        preferred_element_type=jnp.float32,
    )


def apply_cells(
    extended, cell_nodes, scales, stiffness, first_cell, offset_pos, full_len, cell_total
):
    ext_len = extended.shape[1]
    cell_here = cell_nodes.shape[1]
    cell_group = math.gcd(cell_here, 16)
    slide_len = full_len - WINDOW
    window_span = min(ext_len, (cell_group - 1) * slide_len // (cell_total - 1) + WINDOW + 1)
    positions = jnp.arange(window_span, dtype=jnp.int32)

    def one_group(group_index, summed):
        block_first = group_index * cell_group
        seg_start = (first_cell + block_first) * slide_len // (cell_total - 1) - offset_pos
        seg_start = jnp.clip(seg_start, 0, ext_len - window_span).astype(jnp.int32)
        segment = lax.dynamic_slice_in_dim(extended, seg_start, window_span, 1)
        local_nodes = lax.dynamic_slice_in_dim(cell_nodes, block_first, cell_group, 1) - seg_start
        one_hot = (local_nodes[:, :, None] == positions[None, None, :]).astype(jnp.float32)
        values = jnp.einsum("os,kgs->okg", segment, one_hot, precision=lax.Precision.HIGHEST)
        scale_part = lax.dynamic_slice_in_dim(scales, block_first, cell_group, 0)
        images = cell_images(stiffness, values, scale_part)
        added = jnp.einsum("okg,kgs->os", images, one_hot, precision=lax.Precision.HIGHEST)
        previous_sum = lax.dynamic_slice_in_dim(summed, seg_start, window_span, 1)
        return lax.dynamic_update_slice_in_dim(summed, previous_sum + added, seg_start, 1)

    return lax.fori_loop(0, cell_here // cell_group, one_group, jnp.zeros_like(extended))


def body(
    orbitals, others, potential, cell_scale, connectivity, send_up, send_down, stiffness, rotation
):
    band_rows = orbitals.shape[0]
    node_dev = orbitals.shape[1]
    rest_rows = others.shape[0]
    rim_len = send_up.shape[0]
    cell_count = connectivity.shape[1]
    full_len = node_dev + 2 * rim_len
    panel_size = rotation.shape[0]
    band_count = lax.axis_size("band")
    filt_all = band_rows * band_count
    out_rows = panel_size // band_count
    band_pos = lax.axis_index("band")
    columns = lax.dynamic_slice_in_dim(rotation, band_pos * out_rows, out_rows, 1)
    node_line = jnp.arange(node_dev, dtype=jnp.int32)[:, None]
    up_select = (send_up[None, :] == node_line).astype(jnp.float32)
    down_select = (send_down[None, :] == node_line).astype(jnp.float32)

    def operate(vectors):
        up_values = picked(vectors, up_select)
        down_values = picked(vectors, down_select)
        lower_ghost = shifted(up_values, "domain", 1)
        upper_ghost = shifted(down_values, "domain", -1)
        extended = jnp.concatenate([lower_ghost, vectors, upper_ghost], axis=1)
        summed = apply_cells(
            extended, connectivity, cell_scale, stiffness, 0, 0, full_len, cell_count
        )
        owned = summed[:, rim_len : rim_len + node_dev]
        rim_sums = jnp.concatenate([summed[:, :rim_len], summed[:, rim_len + node_dev :]], axis=1)
        returned = with_halo(rim_sums, (("domain", 1),), rim_len)
        from_below = returned[:, :rim_len]
        from_above = returned[:, returned.shape[1] - rim_len :]
        owned = owned + placed(from_below, down_select) + placed(from_above, up_select)
        return owned + potential * vectors

    current = (operate(orbitals) - FILTER_CENTER * orbitals) / FILTER_HALF
    image = operate(current)
    following = 2.0 * (image - FILTER_CENTER * current) / FILTER_HALF - orbitals
    joined = jnp.concatenate([following, others], axis=0)
    local_rows = band_rows + rest_rows
    portion = lax.all_gather(joined, "band", axis=0, tiled=True)
    row_index = jnp.arange(portion.shape[0], dtype=jnp.int32)
    owner_band = row_index // local_rows
    offset_row = row_index % local_rows
    math_row = jnp.where(
        offset_row < band_rows,
        owner_band * band_rows + offset_row,
        filt_all + owner_band * rest_rows + offset_row - band_rows,
    )
    weights = jnp.take(columns, math_row, axis=0)
    return weighted(weights, portion)


def solution(mesh):
    placed = (
        P("band", "domain"),
        P("band", "domain"),
        P("domain"),
        P("domain"),
        P(None, "domain"),
        P("domain"),
        P("domain"),
        P(),
        P(),
    )
    return jax.shard_map(
        body, mesh=mesh, in_specs=placed, out_specs=P("band", "domain"), check_vma=False
    )
```

profile of v0, /device:TPU:1, one launch (start us, length us, event | category | flops | bytes accessed | tf_op | source)
XLA Modules:
  0.0 562.5 jit_solution(13105673384403145671)
XLA Ops:
  6.5 5.4 fusion.42
  12.0 2.8 collective-permute-start
  14.8 4.4 fusion.43
  19.2 11.9 %collective-permute-start.1 = (f32[32,1536]{1,0:T(8,128)S(1)}, f32[32,1536]{1,0:T(8,128)S(1)}, u32[]{:S(2)}, u32[]{:S(2)}) collective-permute-start(f32[32,1536]{1,0:T(8,128)S(1)} %fusion.43), channel_id=1, source_target_pairs={{2,0},{4,2},{6,4},{8,6},{10,8},{12,10},{14,12},{16,14},{18,16},{20... | collective-permute-start | bytes 589832 | tf_op jit(solution)/shard_map/ppermute | solution.py:18
  31.3 4.3 collective-permute-done.1
  35.7 203.6 %while.32 = (s32[]{:T(128)}, f32[32,5120]{1,0:T(8,128)S(1)}, f32[32,5120]{1,0:T(8,128)S(1)}, s32[64,768]{0,1:T(8,128)S(1)}, f32[64,64]{1,0:T(8,128)S(1)}, /*inde...) while((s32[]{:T(128)}, f32[32,5120]{1,0:T(8,128)S(1)}, ...), condition=%wide.region_1.2_spmd.clone, body=%wide.region_0.1_spmd.clone.sunk | while | flops 302755840 | bytes 791037 | solution.py:91
  56.9 1.6 fusion.92
  65.4 1.6 fusion.92
  69.6 1.6 fusion.92
  73.9 1.6 fusion.92
  86.6 1.6 fusion.92
  90.9 1.6 fusion.92
  95.2 1.6 fusion.92
  103.7 1.6 fusion.92
  107.9 1.6 fusion.92
  116.4 1.6 fusion.92
  124.9 1.6 fusion.92
  129.2 1.6 fusion.92
  137.7 1.6 fusion.92
  146.2 1.6 fusion.92
  150.4 1.6 fusion.92
  163.2 1.6 fusion.92
  167.4 1.6 fusion.92
  171.7 1.6 fusion.92
  184.5 1.6 fusion.92
  188.7 1.6 fusion.92
  193.0 1.6 fusion.92
  197.2 1.6 fusion.92
  205.7 1.6 fusion.92
  214.2 1.6 fusion.92
  218.5 1.6 fusion.92
  227.0 1.6 fusion.92
  239.4 5.5 collective-permute-start.3
  246.0 6.1 %fusion.32 = f32[32,2048]{1,0:T(8,128)S(1)} fusion(f32[32,1536]{1,0:T(8,128)S(1)} %collective-permute-done.3, s32[1536]{0:T(1024)S(1)} %copy-done.6), kind=kOutput, calls=%fused_computation.39 | convolution fusion | flops 1211105280 | bytes 464896 | tf_op jit(solution)/shard_map/or,nr->on/dot_general | solution.py:58
  252.1 6.1 %broadcast_multiply_fusion = (f32[32,2048]{1,0:T(8,128)S(1)}, f32[32,2048]{1,0:T(8,128)S(1)}) fusion(f32[32,2048]{1,0:T(8,128)S(1)} %copy-done.3, f32[2048]{0:T(1024)S(1)} %copy-done.5, f32[32,2048]{1,0:T(8,128)S(1)} %fusion.32, f32[32,1536]{1,0:T(8,128)S(1)} %collective-permute-done.2, s32[1536]{0:T(1024)S(1)} %copy-done.7, ...), kind=kOutput, calls=%fused_computation.64 | convolution fusion | flops 1211564032 | bytes 1521664 | tf_op jit(solution)/shard_map/or,nr->on/dot_general | solution.py:58
  258.2 4.9 fusion.31
  263.1 4.5 fusion.27
  267.6 8.3 %collective-permute-start.5 = (f32[32,1536]{1,0:T(8,128)S(1)}, f32[32,1536]{1,0:T(8,128)S(1)}, u32[]{:S(2)}, u32[]{:S(2)}) collective-permute-start(f32[32,1536]{1,0:T(8,128)S(1)} %fusion.27), channel_id=1, source_target_pairs={{2,0},{4,2},{6,4},{8,6},{10,8},{12,10},{14,12},{16,14},{18,16},{20... | collective-permute-start | bytes 589832 | tf_op jit(solution)/shard_map/ppermute | solution.py:18
  277.1 203.6 %while.33 = (s32[]{:T(128)}, f32[32,5120]{1,0:T(8,128)S(1)}, f32[32,5120]{1,0:T(8,128)S(1)}, s32[64,768]{0,1:T(8,128)S(1)}, f32[64,64]{1,0:T(8,128)S(1)}, /*inde...) while((s32[]{:T(128)}, f32[32,5120]{1,0:T(8,128)S(1)}, ...), condition=%wide.region_3.4_spmd.clone, body=%wide.region_2.3_spmd.clone.sunk | while | flops 302755840 | bytes 791037 | solution.py:91
  298.3 1.6 fusion.99
  306.8 1.6 fusion.99
  315.3 1.6 fusion.99
  323.8 1.6 fusion.99
  328.1 1.6 fusion.99
  336.6 1.6 fusion.99
  345.1 1.6 fusion.99
  349.3 1.6 fusion.99
  357.8 1.6 fusion.99
  366.3 1.6 fusion.99
  370.6 1.6 fusion.99
  383.3 1.6 fusion.99
  391.9 1.6 fusion.99
  404.6 1.6 fusion.99
  413.1 1.6 fusion.99
  425.9 1.6 fusion.99
  434.4 1.6 fusion.99
  447.1 1.6 fusion.99
  455.6 1.6 fusion.99
  468.4 1.6 fusion.99
  480.8 8.4 %collective-permute-start.7 = (f32[32,1536]{1,0:T(8,128)S(1)}, f32[32,1536]{1,0:T(8,128)S(1)}, u32[]{:S(2)}, u32[]{:S(2)}) collective-permute-start(f32[32,1536]{1,0:T(8,128)S(1)} %get-tuple-element.440), channel_id=1, source_target_pairs={{2,0},{4,2},{6,4},{8,6},{10,8},{12,10},{14,12},{16,14},{18,16},{20... | collective-permute-start | bytes 589832 | tf_op jit(solution)/shard_map/ppermute | solution.py:30
  490.3 6.1 %fusion.30 = f32[32,2048]{1,0:T(8,128)S(1)} fusion(f32[32,1536]{1,0:T(8,128)S(1)} %collective-permute-done.7, s32[1536]{0:T(1024)S(1)} %copy-done.6), kind=kOutput, calls=%fused_computation.37 | convolution fusion | flops 1211105280 | bytes 464896 | tf_op jit(solution)/shard_map/or,nr->on/dot_general | solution.py:58
  496.4 6.1 %fusion.53 = f32[32,2048]{1,0:T(8,128)S(1)} fusion(f32[32,2048]{1,0:T(8,128)S(1)} %copy-done.3, f32[32,2048]{1,0:T(8,128)S(1)} %get-tuple-element.444, f32[32,2048]{1,0:T(8,128)S(1)} %fusion.30, f32[32,1536]{1,0:T(8,128)S(1)} %collective-permute-done.6, s32[1536]{0:T(1024)S(1)} %copy-done.7, f32[32,5120]{1,0:T(8,128)S(1)} %get-tuple-element.362, ...), kind=kOutput, calls=%fused_computation.60 | convolution fusion | flops 1211564032 | bytes 1521664 | tf_op jit(solution)/shard_map/or,nr->on/dot_general | solution.py:58
  504.4 47.1 %all-gather.2.cloned.1.call-done = f32[256,2048]{1,0:T(8,128)} async-done(((f32[128,2048]{1,0:T(8,128)}), f32[256,2048]{1,0:T(8,128)}) %all-gather.2.cloned.1.call-update) | async-done | bytes 2097168 | tf_op jit(solution)/shard_map/all_gather | solution.py:135
  551.5 3.9 fusion.54
  (572 shorter events, 331.9 us)
Async XLA Ops:
  6.5 497.1 %copy-start = (f32[256,256]{1,0:T(8,128)S(1)}, f32[256,256]{1,0:T(8,128)}, u32[]{:S(2)}) copy-start(f32[256,256]{1,0:T(8,128)} %param.21) | copy-start | bytes 786436
  6.5 8.2 %copy-start.3 = (f32[32,2048]{1,0:T(8,128)S(1)}, f32[32,2048]{1,0:T(8,128)}, u32[]{:S(2)}) copy-start(f32[32,2048]{1,0:T(8,128)} %param.13) | copy-start | bytes 786436
  6.5 8.2 %copy-start.7 = (s32[1536]{0:T(1024)S(1)}, s32[1536]{0:T(1024)}, u32[]{:S(2)}) copy-start(s32[1536]{0:T(1024)} %param.19) | copy-start | bytes 18436
  6.5 545.0 %all-gather.2.cloned.1.call-start = ((), (), s32[]{:S(2)}) async-start(), calls=%async_computation | async-start | bytes 3145728 | tf_op jit(solution)/shard_map/all_gather | solution.py:135
  12.0 19.1 %copy-start.4 = (s32[64,768]{1,0:T(8,128)S(1)}, s32[64,768]{1,0:T(8,128)}, u32[]{:S(2)}) copy-start(s32[64,768]{1,0:T(8,128)} %param.17) | copy-start | bytes 589828
  12.0 19.3 %collective-permute-start = (f32[32,1536]{1,0:T(8,128)S(1)}, f32[32,1536]{1,0:T(8,128)S(1)}, u32[]{:S(2)}, u32[]{:S(2)}) collective-permute-start(f32[32,1536]{1,0:T(8,128)S(1)} %fusion.42), channel_id=1, source_target_pairs={{254,0},{0,2},{2,4},{4,6},{6,8},{8,10},{10,12},{12,14},{14,16},{16... | collective-permute-start | bytes 589832 | tf_op jit(solution)/shard_map/ppermute | solution.py:18
  19.2 16.5 %copy-start.1 = (f32[64,64]{1,0:T(8,128)S(1)}, f32[64,64]{1,0:T(8,128)}, u32[]{:S(2)}) copy-start(f32[64,64]{1,0:T(8,128)} %param.20) | copy-start | bytes 49156
  19.2 16.4 %collective-permute-start.1 = (f32[32,1536]{1,0:T(8,128)S(1)}, f32[32,1536]{1,0:T(8,128)S(1)}, u32[]{:S(2)}, u32[]{:S(2)}) collective-permute-start(f32[32,1536]{1,0:T(8,128)S(1)} %fusion.43), channel_id=1, source_target_pairs={{2,0},{4,2},{6,4},{8,6},{10,8},{12,10},{14,12},{16,14},{18,16},{20... | collective-permute-start | bytes 589832 | tf_op jit(solution)/shard_map/ppermute | solution.py:18
  35.7 210.3 %copy-start.6 = (s32[1536]{0:T(1024)S(1)}, s32[1536]{0:T(1024)}, u32[]{:S(2)}) copy-start(s32[1536]{0:T(1024)} %param.18) | copy-start | bytes 18436
  239.3 12.8 %copy-start.5 = (f32[2048]{0:T(1024)S(1)}, f32[2048]{0:T(1024)}, u32[]{:S(2)}) copy-start(f32[2048]{0:T(1024)} %param.15) | copy-start | bytes 24580
  239.4 6.6 %collective-permute-start.3 = (f32[32,1536]{1,0:T(8,128)S(1)}, f32[32,1536]{1,0:T(8,128)S(1)}, u32[]{:S(2)}, u32[]{:S(2)}) collective-permute-start(f32[32,1536]{1,0:T(8,128)S(1)} %get-tuple-element.442), channel_id=1, source_target_pairs={{2,0},{4,2},{6,4},{8,6},{10,8},{12,10},{14,12},{16,14},{18,16},{20... | collective-permute-start | bytes 589832 | tf_op jit(solution)/shard_map/ppermute | solution.py:30
  244.9 7.2 %collective-permute-start.2 = (f32[32,1536]{1,0:T(8,128)S(1)}, f32[32,1536]{1,0:T(8,128)S(1)}, u32[]{:S(2)}, u32[]{:S(2)}) collective-permute-start(f32[32,1536]{1,0:T(8,128)S(1)} %get-tuple-element.441), channel_id=1, source_target_pairs={{0,2},{2,4},{4,6},{6,8},{8,10},{10,12},{12,14},{14,16},{16,18},{18... | collective-permute-start | bytes 589832 | tf_op jit(solution)/shard_map/ppermute | solution.py:28
  267.6 9.3 %collective-permute-start.4 = (f32[32,1536]{1,0:T(8,128)S(1)}, f32[32,1536]{1,0:T(8,128)S(1)}, u32[]{:S(2)}, u32[]{:S(2)}) collective-permute-start(f32[32,1536]{1,0:T(8,128)S(1)} %fusion.31), channel_id=1, source_target_pairs={{254,0},{0,2},{2,4},{4,6},{6,8},{8,10},{10,12},{12,14},{14,16},{16... | collective-permute-start | bytes 589832 | tf_op jit(solution)/shard_map/ppermute | solution.py:18
  267.6 9.4 %collective-permute-start.5 = (f32[32,1536]{1,0:T(8,128)S(1)}, f32[32,1536]{1,0:T(8,128)S(1)}, u32[]{:S(2)}, u32[]{:S(2)}) collective-permute-start(f32[32,1536]{1,0:T(8,128)S(1)} %fusion.27), channel_id=1, source_target_pairs={{2,0},{4,2},{6,4},{8,6},{10,8},{12,10},{14,12},{16,14},{18,16},{20... | collective-permute-start | bytes 589832 | tf_op jit(solution)/shard_map/ppermute | solution.py:18
  480.8 9.5 %collective-permute-start.7 = (f32[32,1536]{1,0:T(8,128)S(1)}, f32[32,1536]{1,0:T(8,128)S(1)}, u32[]{:S(2)}, u32[]{:S(2)}) collective-permute-start(f32[32,1536]{1,0:T(8,128)S(1)} %get-tuple-element.440), channel_id=1, source_target_pairs={{2,0},{4,2},{6,4},{8,6},{10,8},{12,10},{14,12},{16,14},{18,16},{20... | collective-permute-start | bytes 589832 | tf_op jit(solution)/shard_map/ppermute | solution.py:30
  489.2 7.2 %collective-permute-start.6 = (f32[32,1536]{1,0:T(8,128)S(1)}, f32[32,1536]{1,0:T(8,128)S(1)}, u32[]{:S(2)}, u32[]{:S(2)}) collective-permute-start(f32[32,1536]{1,0:T(8,128)S(1)} %get-tuple-element.439), channel_id=1, source_target_pairs={{0,2},{2,4},{4,6},{6,8},{8,10},{10,12},{12,14},{14,16},{16,18},{18... | collective-permute-start | bytes 589832 | tf_op jit(solution)/shard_map/ppermute | solution.py:28
  496.4 6.1 %copy-start.2 = (f32[96,2048]{1,0:T(8,128)S(1)}, f32[96,2048]{1,0:T(8,128)}, u32[]{:S(2)}) copy-start(f32[96,2048]{1,0:T(8,128)} %param.14) | copy-start | bytes 2359300
Sparse Core Ops, SparseCore 0:
  503.7 47.7 all-gather.1
where the time goes:
time: 573 us; the launch traced here: 562 us
  matrix products  304 us (53%)
  local copies, waits for them, and re-layouts  143 us (25%)
  waiting for transfers between devices  54.5 us (10%)
  starting transfers between devices  37.1 us (6%)
  between operations  13.8 us (2%)
  loops' own time  7.12 us (1%)
    dot_general x96, matrix products, one_group(): jnp.einsum('os,kgs->okg', segment, one_hot, precision=lax.Precision.HIGHEST)  154 us
    dynamic_slice x96, local copies, waits for them, and re-layouts, one_group(): scale_part = lax.dynamic_slice_in_dim(scales, block_first, cell_group, 0)  73.6 us
    dynamic_update_slice x96, local copies, waits for them, and re-layouts, one_group(): lax.dynamic_update_slice_in_dim(summed, previous_sum + added, seg_start, 1)  68.7 us
    dot_general x96, matrix products, one_group(): jnp.einsum('okg,kgs->os', images, one_hot, precision=lax.Precision.HIGHEST)  67.8 us
    all_gather x1, waiting for transfers between devices, body(): portion = lax.all_gather(joined, 'band', axis=0, tiled=True)  47.1 us
    dot_general x96, matrix products, cell_images(): jnp.einsum('ij,ojc->oic', stiffness, values, precision=lax.Precision.HIGH...  35 us
    dot_general x4, matrix products, placed(): jnp.einsum('or,nr->on', values, selector, precision=lax.Precision.HIGHEST...  24.4 us
    ppermute x4, starting transfers between devices, shifted(): return lax.ppermute(block, axis, route)  23.1 us
  transfers between devices with their start and end apart: 9, of which 6 were waited for; matrix products, arithmetic and copies ran while one was open for 3% of the time, Pallas kernels for 0%

commit v1 on v0

v1 whole, which is shorter than its diff:
```python
import functools

import jax
import jax.numpy as jnp
from jax import lax
from jax.experimental import pallas as pl
from jax.experimental.pallas import tpu as pltpu
from jax.sharding import PartitionSpec as P

bf16 = jnp.bfloat16
f32 = jnp.float32
MESH = pl.DeviceIdType.MESH

WINDOW = 256
CENTER = 64.0
HALF = 64.0

GROUP = 16
PAIRS = GROUP // 2
SPAN = 512


def split(values):
    high = values.astype(bf16)
    return high, (values - high.astype(f32)).astype(bf16)


def group_base(g, cells, ext_len):
    first = (GROUP * g * (ext_len - WINDOW)) // (cells - 1)
    return pl.multiple_of(jnp.minimum((first // 128) * 128, ext_len - SPAN), 128)


def list_one_hot(list_ref, one_hot):
    lanes = lax.broadcasted_iota(jnp.int32, (256, 128), 0)
    for j in range(list_ref.shape[0]):
        entry = jnp.broadcast_to(list_ref[j : j + 1, :] & 255, (256, 128))
        one_hot[:, 128 * j : 128 * j + 128] = jnp.where(lanes == entry, 1.0, 0.0).astype(bf16)


def pick(source, list_ref, one_hot, target):
    rows, nodes = source.shape
    blocks = nodes // 256
    parts = [split(source[:, 256 * k : 256 * k + 256]) for k in range(blocks)]
    left = jnp.concatenate([p[0] for p in parts] + [p[1] for p in parts], axis=0)
    for j in range(list_ref.shape[0] // 2):
        both = jnp.dot(left, one_hot[:, 256 * j : 256 * j + 256], preferred_element_type=f32)
        block = jnp.concatenate([list_ref[2 * j : 2 * j + 1, :], list_ref[2 * j + 1 : 2 * j + 2, :]], axis=1) >> 8
        block = jnp.broadcast_to(block, (rows, 256))
        total = jnp.zeros((rows, 256), f32)
        for k in range(blocks):
            here = both[rows * k : rows * k + rows] + both[rows * (blocks + k) : rows * (blocks + k) + rows]
            total = jnp.where(block == k, here, total)
        target[:, 256 * j : 256 * j + 256] = total


def place(source, list_ref, one_hot, target):
    rows, nodes = target.shape
    blocks = nodes // 256
    entries = source.shape[1]
    columns = []
    for j in range(entries // 128):
        values = source[:, 128 * j : 128 * j + 128]
        high = values.astype(bf16).astype(f32)
        low = values - high
        block = jnp.broadcast_to(list_ref[j : j + 1, :] >> 8, (rows, 128))
        zero = jnp.zeros_like(values)
        masks = [block == k for k in range(blocks)]
        columns.append(
            jnp.concatenate(
                [jnp.where(m, high, zero) for m in masks] + [jnp.where(m, low, zero) for m in masks], axis=0
            ).astype(bf16)
        )
    left = jnp.concatenate(columns, axis=1)
    both = lax.dot_general(left, one_hot[...], (((1,), (1,)), ((), ())), preferred_element_type=f32)
    for k in range(blocks):
        here = both[rows * k : rows * k + rows] + both[rows * (blocks + k) : rows * (blocks + k) + rows]
        target[:, 256 * k : 256 * k + 256] += here


def build_stiffness(stiffness, paired):
    high, low = split(stiffness[...])
    none = jnp.zeros_like(high)
    rows = [[high, none, low, none], [none, high, none, low], [high, none, none, none], [none, high, none, none]]
    paired[...] = jnp.concatenate([jnp.concatenate(row, axis=1) for row in rows], axis=0)


def build_cells(index_ref, one_hot, cells, ext_len):
    def step(g, carry):
        base = group_base(g, cells, ext_len)
        local = (index_ref[pl.ds(pl.multiple_of(PAIRS * g, PAIRS), PAIRS), :] - base) & 255
        lanes = lax.broadcasted_iota(jnp.int32, (256, 128), 0)
        for h in range(PAIRS):
            entry = jnp.broadcast_to(local[h : h + 1, :], (256, 128))
            one_hot[g, 128 * h : 128 * h + 128, :] = jnp.where(lanes == entry, 1.0, 0.0).astype(bf16).T
        return carry

    lax.fori_loop(0, cells // GROUP, step, 0, unroll=2)


def run_cells(first, last, unroll, extended, index_ref, scale_ref, pair_stiffness, one_hot, summed):
    rows, ext_len = extended.shape
    cells = 2 * index_ref.shape[0]
    row_tiles = rows // 8

    def step(g, carry):
        base = group_base(g, cells, ext_len)
        source = [
            [extended[8 * o : 8 * o + 8, pl.ds(base + 128 * k, 128)] for k in range(4)] for o in range(row_tiles)
        ]
        at = pl.multiple_of(PAIRS * g, PAIRS)
        local = index_ref[pl.ds(at, PAIRS), :] - base
        scales = scale_ref[pl.ds(at, PAIRS), :]
        values, upper = [], []
        for h in range(PAIRS):
            position = jnp.broadcast_to(local[h : h + 1, :], (8, 128))
            block, lane = position >> 7, position & 127
            tiles = []
            for o in range(row_tiles):
                tile = jnp.take_along_axis(source[o][0], lane, axis=1)
                for k in range(1, 4):
                    tile = jnp.where(block == k, jnp.take_along_axis(source[o][k], lane, axis=1), tile)
                tiles.append(tile)
            values.append(jnp.concatenate(split(jnp.concatenate(tiles, axis=0)), axis=1))
            upper.append(jnp.concatenate([block] * row_tiles, axis=0) >= 2)
        images = jnp.dot(jnp.concatenate(values, axis=0), pair_stiffness[...], preferred_element_type=f32)
        images = images[:, :128] + images[:, 128:]
        columns = []
        for h in range(PAIRS):
            image = images[rows * h : rows * h + rows] * jnp.broadcast_to(scales[h : h + 1, :], (rows, 128))
            high = image.astype(bf16).astype(f32)
            low = image - high
            zero = jnp.zeros_like(image)
            columns.append(
                jnp.concatenate(
                    [
                        jnp.where(upper[h], zero, high),
                        jnp.where(upper[h], high, zero),
                        jnp.where(upper[h], zero, low),
                        jnp.where(upper[h], low, zero),
                    ],
                    axis=0,
                ).astype(bf16)
            )
        left = jnp.concatenate(columns, axis=1)
        both = jnp.dot(left, one_hot[g], preferred_element_type=f32)
        added = both[: 2 * rows] + both[2 * rows :]
        summed[:, pl.ds(base, 256)] += added[:rows]
        summed[:, pl.ds(base + 256, 256)] += added[rows:]
        return carry

    lax.fori_loop(first, last, step, 0, unroll=unroll)


def kernel(
    n_domain,
    orbitals,
    others,
    potential,
    index_ref,
    scale_ref,
    up_list,
    down_list,
    stiffness,
    rotation,
    out,
    pair_stiffness,
    one_hot,
    up_hot,
    down_hot,
    extended,
    sums,
    up_out,
    down_out,
    up_back,
    down_back,
    current,
    panel,
    others_sems,
    ghost_send,
    ghost_recv,
    back_send,
    back_recv,
    filt_sems,
):
    rows, nodes = orbitals.shape
    rim = up_out.shape[2]
    ext_len = extended.shape[2]
    cells = 2 * index_ref.shape[0]
    groups = cells // GROUP
    low_end = 288 // GROUP
    high_start = groups - low_end
    rest = others.shape[0]
    half = out.shape[0]

    me = lax.axis_index("domain")
    band = lax.axis_index("band")
    above, below = lax.rem(me + 1, n_domain), lax.rem(me + n_domain - 1, n_domain)
    mate = 1 - band

    barrier = pltpu.get_barrier_semaphore()
    for target in ({"domain": above}, {"domain": below}, {"band": mate}):
        pl.semaphore_signal(barrier, inc=1, device_id=target, device_id_type=MESH)

    other_rows = pl.ds(pl.multiple_of(2 * rows + rest * band, 8), rest)
    own_others = pltpu.make_async_copy(others, panel.at[other_rows, :], others_sems.at[0])
    own_others.start()
    build_stiffness(stiffness, pair_stiffness)
    list_one_hot(up_list, up_hot)
    list_one_hot(down_list, down_hot)

    def send_ghosts(source, step):
        pick(source, up_list, up_hot, up_out.at[step])
        up = pltpu.make_async_remote_copy(
            src_ref=up_out.at[step],
            dst_ref=extended.at[step, :, pl.ds(0, rim)],
            send_sem=ghost_send.at[step, 0],
            recv_sem=ghost_recv.at[step, 0],
            device_id={"domain": above},
            device_id_type=MESH,
        )
        if step == 0:
            pl.semaphore_wait(barrier, 3)
        up.start()
        pick(source, down_list, down_hot, down_out.at[step])
        down = pltpu.make_async_remote_copy(
            src_ref=down_out.at[step],
            dst_ref=extended.at[step, :, pl.ds(rim + nodes, rim)],
            send_sem=ghost_send.at[step, 1],
            recv_sem=ghost_recv.at[step, 1],
            device_id={"domain": below},
            device_id_type=MESH,
        )
        down.start()
        extended[step, :, rim : rim + nodes] = source[...]
        sums[step] = jnp.zeros((rows, ext_len), f32)
        return up, down

    def send_back(step, lower):
        copy = pltpu.make_async_remote_copy(
            src_ref=sums.at[step, :, pl.ds(0 if lower else rim + nodes, rim)],
            dst_ref=(up_back if lower else down_back).at[step],
            send_sem=back_send.at[step, 0 if lower else 1],
            recv_sem=back_recv.at[step, 0 if lower else 1],
            device_id={"domain": below if lower else above},
            device_id_type=MESH,
        )
        copy.start()
        return copy

    def cells_from(step, first, last, unroll):
        run_cells(
            first,
            last,
            unroll,
            extended.at[step],
            index_ref,
            scale_ref,
            pair_stiffness,
            one_hot,
            sums.at[step],
        )

    def operate(step, ghosts):
        up, down = ghosts
        up.wait()
        cells_from(step, 0, low_end, 6)
        lower = send_back(step, True)
        down.wait()
        cells_from(step, high_start, groups, 6)
        upper = send_back(step, False)
        cells_from(step, low_end, high_start, 6)
        return lower, upper

    def collect(step, backs, target):
        lower, upper = backs
        target[...] = sums[step, :, rim : rim + nodes]
        lower.wait()
        place(up_back.at[step], up_list, up_hot, target)
        upper.wait()
        place(down_back.at[step], down_list, down_hot, target)

    ghosts = send_ghosts(orbitals, 0)
    mate_others = pltpu.make_async_remote_copy(
        src_ref=others,
        dst_ref=panel.at[other_rows, :],
        send_sem=others_sems.at[1],
        recv_sem=others_sems.at[2],
        device_id={"band": mate},
        device_id_type=MESH,
    )
    mate_others.start()
    build_cells(index_ref, one_hot, cells, ext_len)
    backs = operate(0, ghosts)
    collect(0, backs, current)
    current[...] = (current[...] + potential[...] * orbitals[...] - CENTER * orbitals[...]) * (1.0 / HALF)
    ghosts = send_ghosts(current, 1)
    backs = operate(1, ghosts)

    mine = pl.ds(pl.multiple_of(rows * band, 8), rows)
    collect(1, backs, panel.at[mine, :])
    for k in range(nodes // 256):
        cut = slice(256 * k, 256 * k + 256)
        now = current[:, cut]
        panel[mine, cut] = (
            panel[mine, cut] + potential[:, cut] * now - CENTER * now
        ) * (2.0 / HALF) - orbitals[:, cut]
    mate_filt = pltpu.make_async_remote_copy(
        src_ref=panel.at[mine, :],
        dst_ref=panel.at[mine, :],
        send_sem=filt_sems.at[0],
        recv_sem=filt_sems.at[1],
        device_id={"band": mate},
        device_id_type=MESH,
    )
    mate_filt.start()
    own_others.wait()
    mate_others.wait()
    mate_filt.wait()
    weights = rotation[:, pl.ds(pl.multiple_of(band * half, 128), half)].T
    left = jnp.concatenate(split(weights), axis=0)
    for k in range(nodes // 256):
        cut = slice(256 * k, 256 * k + 256)
        high, low = split(panel[:, cut])
        main = jnp.dot(left, high, preferred_element_type=f32)
        out[:, cut] = main[:half] + main[half:] + jnp.dot(left[:half], low, preferred_element_type=f32)


def body(
    orbitals, others, potential, cell_scale, connectivity, send_up, send_down, stiffness, rotation
):
    rows, nodes = orbitals.shape
    rest = others.shape[0]
    rim = send_up.shape[0]
    npc, cells = connectivity.shape
    ext_len = nodes + 2 * rim
    panel = rotation.shape[0]
    half = panel // lax.axis_size("band")
    index = connectivity.T.reshape(cells // 2, 2 * npc)
    scale = jnp.repeat(cell_scale, npc).reshape(cells // 2, 2 * npc)
    vmem = pl.BlockSpec(memory_space=pltpu.VMEM)
    return pl.pallas_call(
        functools.partial(kernel, lax.axis_size("domain")),
        out_shape=jax.ShapeDtypeStruct((half, nodes), f32),
        in_specs=[vmem, pl.BlockSpec(memory_space=pl.ANY)] + [vmem] * 7,
        out_specs=vmem,
        scratch_shapes=[
            pltpu.VMEM((4 * npc, 4 * npc), bf16),
            pltpu.VMEM((cells // GROUP, GROUP * npc, 256), bf16),
            pltpu.VMEM((256, rim), bf16),
            pltpu.VMEM((256, rim), bf16),
            pltpu.VMEM((2, rows, ext_len), f32),
            pltpu.VMEM((2, rows, ext_len), f32),
            pltpu.VMEM((2, rows, rim), f32),
            pltpu.VMEM((2, rows, rim), f32),
            pltpu.VMEM((2, rows, rim), f32),
            pltpu.VMEM((2, rows, rim), f32),
            pltpu.VMEM((rows, nodes), f32),
            pltpu.VMEM((panel, nodes), f32),
            pltpu.SemaphoreType.DMA((3,)),
            pltpu.SemaphoreType.DMA((2, 2)),
            pltpu.SemaphoreType.DMA((2, 2)),
            pltpu.SemaphoreType.DMA((2, 2)),
            pltpu.SemaphoreType.DMA((2, 2)),
            pltpu.SemaphoreType.DMA((2,)),
        ],
        compiler_params=pltpu.CompilerParams(
            collective_id=0, has_side_effects=True, vmem_limit_bytes=52 * 2**20
        ),
        name="filter_rotate",
    )(
        orbitals,
        others,
        potential.reshape(1, nodes),
        index,
        scale,
        send_up.reshape(rim // 128, 128),
        send_down.reshape(rim // 128, 128),
        stiffness,
        rotation,
    )


def solution(mesh):
    placed = (
        P("band", "domain"),
        P("band", "domain"),
        P("domain"),
        P("domain"),
        P(None, "domain"),
        P("domain"),
        P("domain"),
        P(),
        P(),
    )
    return jax.shard_map(
        body, mesh=mesh, in_specs=placed, out_specs=P("band", "domain"), check_vma=False
    )
```

time: 573 us -> 68.4 us (0.12)
  the two profiles are of different devices: /device:TPU:1 before, /device:TPU:193 now
where the time goes in v1:
time: 68.4 us; the launch traced here: 68.2 us
  Pallas kernels  62.8 us (92%)
  local copies, waits for them, and re-layouts  5.34 us (8%)
    pallas_call x1, Pallas kernels, body(): pl.pallas_call(functools.partial(kernel, lax.axis_size('domain')), out_sh...  62.8 us
    unnamed x19, local copies, waits for them, and re-layouts  4.66 us

profile of v1, /device:TPU:193, one launch (start us, length us, event | category | flops | bytes accessed | tf_op | source)
XLA Modules:
  0.0 68.2 jit_solution(11777034491806401062)
XLA Ops:
  0.0 0.0 copy-start.8
  0.0 0.7 %copy-done.8 = f32[768]{0:T(1024)S(1)} copy-done((f32[768]{0:T(1024)S(1)}, f32[768]{0:T(1024)}, u32[]{:S(2)}) %copy-start.8) | copy-done | bytes 3096
  0.7 0.2 broadcast_in_dim.7
  0.9 0.1 copy.12
  0.9 0.0 copy-start.7
  1.0 0.0 copy-start
  1.0 0.1 copy.13.scale_ref
  1.1 0.8 %copy-done.7 = s32[64,768]{1,0:T(8,128)S(1)} copy-done((s32[64,768]{1,0:T(8,128)S(1)}, s32[64,768]{1,0:T(8,128)}, u32[]{:S(2)}) %copy-start.7) | copy-done | bytes 196632
  1.9 0.2 copy.11
  2.1 0.0 copy-start.1
  2.1 0.0 copy-start.2
  2.1 0.0 copy-start.3
  2.1 0.0 copy-start.4
  2.1 0.0 copy-start.5
  2.1 0.0 copy-start.6
  2.1 0.1 reshape.15.index_ref
  2.3 0.0 copy-done
  2.3 0.8 %copy-done.1 = f32[32,2048]{1,0:T(8,128)S(1)} copy-done((f32[32,2048]{1,0:T(8,128)S(1)}, f32[32,2048]{1,0:T(8,128)}, u32[]{:S(2)}) %copy-start.1) | copy-done | bytes 262168
  3.1 0.1 copy-done.2
  3.1 0.0 copy-done.3
  3.1 0.0 copy-done.4
  3.1 0.0 copy-done.5
  3.1 0.0 copy-done.6
  3.2 62.8 %filter_rotate.1 = f32[128,2048]{1,0:T(8,128)} custom-call(f32[32,2048]{1,0:T(8,128)S(1)} %copy-done.1, f32[96,2048]{1,0:T(8,128)S(1)} %copy-done, f32[1,2048]{1,0:T(1,128)S(1)} %bitcast.5, s32[384,128]{1,0:T(8,128)S(1)} %reshape.15.index_ref, f32[384,128]{1,0:T(8,128)S(1)} %copy.13.scale_ref, s32[12,128]{1,0:T(8,128)S(1)} %bitcast.6, ...), custom_call_target="tpu_custom_call" | custom-call | tf_op jit(solution)/shard_map/filter_rotate/pallas_call | solution.py:341
  65.9 2.3 %copy.15 = f32[128,2048]{1,0:T(8,128)} copy(f32[128,2048]{1,0:T(8,128)} %filter_rotate.1) | data formatting | bytes 2097152
  (1 shorter events, 0.0 us)
Async XLA Ops:
  0.0 0.7 %copy-start.8 = (f32[768]{0:T(1024)S(1)}, f32[768]{0:T(1024)}, u32[]{:S(2)}) copy-start(f32[768]{0:T(1024)} %param.12) | copy-start | bytes 9220
  0.9 1.0 %copy-start.7 = (s32[64,768]{1,0:T(8,128)S(1)}, s32[64,768]{1,0:T(8,128)}, u32[]{:S(2)}) copy-start(s32[64,768]{1,0:T(8,128)} %param.13) | copy-start | bytes 589828
  1.0 1.3 %copy-start = (f32[96,2048]{1,0:T(8,128)S(1)}, f32[96,2048]{1,0:T(8,128)}, u32[]{:S(2)}) copy-start(f32[96,2048]{1,0:T(8,128)} %others.1) | copy-start | bytes 2359300
  2.1 1.0 %copy-start.1 = (f32[32,2048]{1,0:T(8,128)S(1)}, f32[32,2048]{1,0:T(8,128)}, u32[]{:S(2)}) copy-start(f32[32,2048]{1,0:T(8,128)} %orbitals.1) | copy-start | bytes 786436
  2.1 1.1 %copy-start.2 = (f32[256,256]{1,0:T(8,128)S(1)}, f32[256,256]{1,0:T(8,128)}, u32[]{:S(2)}) copy-start(f32[256,256]{1,0:T(8,128)} %rotation.1) | copy-start | bytes 786436
  2.1 1.0 %copy-start.3 = (f32[64,64]{1,0:T(8,128)S(1)}, f32[64,64]{1,0:T(8,128)}, u32[]{:S(2)}) copy-start(f32[64,64]{1,0:T(8,128)} %stiffness.1) | copy-start | bytes 49156
  2.1 1.0 %copy-start.4 = (f32[2048]{0:T(1024)S(1)}, f32[2048]{0:T(1024)}, u32[]{:S(2)}) copy-start(f32[2048]{0:T(1024)} %param.11) | copy-start | bytes 24580
  2.1 1.0 %copy-start.5 = (s32[1536]{0:T(1024)S(1)}, s32[1536]{0:T(1024)}, u32[]{:S(2)}) copy-start(s32[1536]{0:T(1024)} %param.14) | copy-start | bytes 18436
  2.1 1.0 %copy-start.6 = (s32[1536]{0:T(1024)S(1)}, s32[1536]{0:T(1024)}, u32[]{:S(2)}) copy-start(s32[1536]{0:T(1024)} %param.15) | copy-start | bytes 18436

commit v2 on v1

--- a/solution.py
+++ b/solution.py
@@ -151,13 +151,28 @@
     lax.fori_loop(first, last, step, 0, unroll=unroll)
 
 
+def pair_rows(block, turn, target):
+    turn[...] = jnp.concatenate([block, pltpu.roll(block, 127, 1)], axis=0).T
+    target[...] = turn[pl.ds(0, 64, stride=2), :]
+
+
+def pieces(weights):
+    high, low = split(weights)
+    return jnp.concatenate([high, high, low], axis=1)
+
+
+def times(weights, values):
+    high, low = split(values)
+    return jnp.dot(weights, jnp.concatenate([high, low, high], axis=0), preferred_element_type=f32)
+
+
 def kernel(
     n_domain,
     orbitals,
     others,
     potential,
-    index_ref,
-    scale_ref,
+    connectivity,
+    cell_scale,
     up_list,
     down_list,
     stiffness,
@@ -167,6 +182,10 @@
     one_hot,
     up_hot,
     down_hot,
+    index_ref,
+    scale_ref,
+    index_turn,
+    scale_turn,
     extended,
     sums,
     up_out,
@@ -174,23 +193,32 @@
     up_back,
     down_back,
     current,
-    panel,
-    others_sems,
+    own_others,
+    mate_others,
+    own_filt,
+    mate_filt,
+    rotated,
+    own_sem,
+    others_send,
+    others_recv,
     ghost_send,
     ghost_recv,
     back_send,
     back_recv,
-    filt_sems,
+    filt_send,
+    filt_recv,
+    out_sems,
 ):
     rows, nodes = orbitals.shape
     rim = up_out.shape[2]
     ext_len = extended.shape[2]
-    cells = 2 * index_ref.shape[0]
+    cells = connectivity.shape[1]
     groups = cells // GROUP
     low_end = 288 // GROUP
     high_start = groups - low_end
     rest = others.shape[0]
     half = out.shape[0]
+    piece = nodes // filt_send.shape[0]
 
     me = lax.axis_index("domain")
     band = lax.axis_index("band")
@@ -201,10 +229,8 @@
     for target in ({"domain": above}, {"domain": below}, {"band": mate}):
         pl.semaphore_signal(barrier, inc=1, device_id=target, device_id_type=MESH)
 
-    other_rows = pl.ds(pl.multiple_of(2 * rows + rest * band, 8), rest)
-    own_others = pltpu.make_async_copy(others, panel.at[other_rows, :], others_sems.at[0])
-    own_others.start()
-    build_stiffness(stiffness, pair_stiffness)
+    own_copy = pltpu.make_async_copy(others, own_others, own_sem)
+    own_copy.start()
     list_one_hot(up_list, up_hot)
     list_one_hot(down_list, down_hot)
 
@@ -247,6 +273,19 @@
         copy.start()
         return copy
 
+    def send_others(step):
+        cut = pl.ds(0, rest // 3 * 2) if step == 0 else pl.ds(rest // 3 * 2, rest // 3)
+        copy = pltpu.make_async_remote_copy(
+            src_ref=own_others.at[cut, :],
+            dst_ref=mate_others.at[cut, :],
+            send_sem=others_send.at[step],
+            recv_sem=others_recv.at[step],
+            device_id={"band": mate},
+            device_id_type=MESH,
+        )
+        copy.start()
+        return copy
+
     def cells_from(step, first, last, unroll):
         run_cells(
             first,
@@ -260,69 +299,103 @@
             sums.at[step],
         )
 
-    def operate(step, ghosts):
-        up, down = ghosts
-        up.wait()
-        cells_from(step, 0, low_end, 6)
-        lower = send_back(step, True)
-        down.wait()
-        cells_from(step, high_start, groups, 6)
-        upper = send_back(step, False)
-        cells_from(step, low_end, high_start, 6)
-        return lower, upper
-
-    def collect(step, backs, target):
-        lower, upper = backs
-        target[...] = sums[step, :, rim : rim + nodes]
-        lower.wait()
-        place(up_back.at[step], up_list, up_hot, target)
-        upper.wait()
-        place(down_back.at[step], down_list, down_hot, target)
-
-    ghosts = send_ghosts(orbitals, 0)
-    mate_others = pltpu.make_async_remote_copy(
-        src_ref=others,
-        dst_ref=panel.at[other_rows, :],
-        send_sem=others_sems.at[1],
-        recv_sem=others_sems.at[2],
-        device_id={"band": mate},
-        device_id_type=MESH,
-    )
-    mate_others.start()
+    up, down = send_ghosts(orbitals, 0)
+    build_stiffness(stiffness, pair_stiffness)
+    for k in range(cells // 128):
+        cut = slice(128 * k, 128 * k + 128)
+        pair_rows(connectivity[:, cut], index_turn, index_ref.at[64 * k : 64 * k + 64, :])
+        pair_rows(
+            jnp.broadcast_to(cell_scale[k : k + 1, :], (64, 128)), scale_turn, scale_ref.at[64 * k : 64 * k + 64, :]
+        )
     build_cells(index_ref, one_hot, cells, ext_len)
-    backs = operate(0, ghosts)
-    collect(0, backs, current)
-    current[...] = (current[...] + potential[...] * orbitals[...] - CENTER * orbitals[...]) * (1.0 / HALF)
-    ghosts = send_ghosts(current, 1)
-    backs = operate(1, ghosts)
-
-    mine = pl.ds(pl.multiple_of(rows * band, 8), rows)
-    collect(1, backs, panel.at[mine, :])
+    own_copy.wait()
+    up.wait()
+    others_0 = send_others(0)
+    cells_from(0, 0, low_end, 9)
+    lower = send_back(0, True)
+    down.wait()
+    cells_from(0, high_start, groups, 9)
+    upper = send_back(0, False)
+    cells_from(0, low_end, high_start, 6)
+    current[...] = sums[0, :, rim : rim + nodes]
+    lower.wait()
+    place(up_back.at[0], up_list, up_hot, current)
+    upper.wait()
+    place(down_back.at[0], down_list, down_hot, current)
     for k in range(nodes // 256):
         cut = slice(256 * k, 256 * k + 256)
+        before = orbitals[:, cut]
+        current[:, cut] = (current[:, cut] + potential[:, cut] * before - CENTER * before) * (1.0 / HALF)
+
+    up, down = send_ghosts(current, 1)
+    cells_from(1, low_end, high_start, 6)
+    up.wait()
+    others_1 = send_others(1)
+    cells_from(1, 0, low_end, 9)
+    lower = send_back(1, True)
+    down.wait()
+    cells_from(1, high_start, groups, 9)
+    upper = send_back(1, False)
+    own_filt[...] = sums[1, :, rim : rim + nodes]
+
+    columns = pl.ds(pl.multiple_of(band * half, 128), half)
+
+    def weights_of(first, count):
+        return rotation[pl.ds(pl.multiple_of(first, 8), count), columns].T
+
+    others_0.wait()
+    others_1.wait()
+    high, low = split(
+        jnp.concatenate([weights_of(2 * rows + rest * band, rest), weights_of(2 * rows + rest * mate, rest)], axis=1)
+    )
+    both_parts = jnp.concatenate([high, low], axis=0)
+
+    def other_products(k, carry):
+        cut = pl.ds(pl.multiple_of(256 * k, 256), 256)
+        high_values, low_values = split(jnp.concatenate([own_others[:, cut], mate_others[:, cut]], axis=0))
+        main = jnp.dot(both_parts, high_values, preferred_element_type=f32)
+        rotated[:, cut] = main[:half] + main[half:] + jnp.dot(high, low_values, preferred_element_type=f32)
+        return carry
+
+    lax.fori_loop(0, nodes // 256, other_products, 0, unroll=2)
+    own_weights = pieces(weights_of(rows * band, rows))
+    mate_weights = pieces(weights_of(rows * mate, rows))
+
+    lower.wait()
+    place(up_back.at[1], up_list, up_hot, own_filt)
+    upper.wait()
+    place(down_back.at[1], down_list, down_hot, own_filt)
+    copies = []
+    for k in range(nodes // piece):
+        cut = slice(piece * k, piece * k + piece)
         now = current[:, cut]
-        panel[mine, cut] = (
-            panel[mine, cut] + potential[:, cut] * now - CENTER * now
-        ) * (2.0 / HALF) - orbitals[:, cut]
-    mate_filt = pltpu.make_async_remote_copy(
-        src_ref=panel.at[mine, :],
-        dst_ref=panel.at[mine, :],
-        send_sem=filt_sems.at[0],
-        recv_sem=filt_sems.at[1],
-        device_id={"band": mate},
-        device_id_type=MESH,
-    )
-    mate_filt.start()
-    own_others.wait()
-    mate_others.wait()
-    mate_filt.wait()
-    weights = rotation[:, pl.ds(pl.multiple_of(band * half, 128), half)].T
-    left = jnp.concatenate(split(weights), axis=0)
+        own_filt[:, cut] = (own_filt[:, cut] + potential[:, cut] * now - CENTER * now) * (2.0 / HALF) - orbitals[:, cut]
+        copy = pltpu.make_async_remote_copy(
+            src_ref=own_filt.at[:, pl.ds(piece * k, piece)],
+            dst_ref=mate_filt.at[:, pl.ds(piece * k, piece)],
+            send_sem=filt_send.at[k],
+            recv_sem=filt_recv.at[k],
+            device_id={"band": mate},
+            device_id_type=MESH,
+        )
+        copy.start()
+        copies.append(copy)
     for k in range(nodes // 256):
         cut = slice(256 * k, 256 * k + 256)
-        high, low = split(panel[:, cut])
-        main = jnp.dot(left, high, preferred_element_type=f32)
-        out[:, cut] = main[:half] + main[half:] + jnp.dot(left[:half], low, preferred_element_type=f32)
+        rotated[:, cut] += times(own_weights, own_filt[:, cut])
+    writes = []
+    for k in range(nodes // piece):
+        copies[k].wait()
+        for j in range(piece // 256):
+            cut = slice(piece * k + 256 * j, piece * k + 256 * j + 256)
+            rotated[:, cut] += times(mate_weights, mate_filt[:, cut])
+        write = pltpu.make_async_copy(
+            rotated.at[:, pl.ds(piece * k, piece)], out.at[:, pl.ds(piece * k, piece)], out_sems.at[k]
+        )
+        write.start()
+        writes.append(write)
+    for write in writes:
+        write.wait()
 
 
 def body(
@@ -335,19 +408,23 @@
     ext_len = nodes + 2 * rim
     panel = rotation.shape[0]
     half = panel // lax.axis_size("band")
-    index = connectivity.T.reshape(cells // 2, 2 * npc)
-    scale = jnp.repeat(cell_scale, npc).reshape(cells // 2, 2 * npc)
+    parts = 4
     vmem = pl.BlockSpec(memory_space=pltpu.VMEM)
+    hbm = pl.BlockSpec(memory_space=pl.ANY)
     return pl.pallas_call(
         functools.partial(kernel, lax.axis_size("domain")),
         out_shape=jax.ShapeDtypeStruct((half, nodes), f32),
-        in_specs=[vmem, pl.BlockSpec(memory_space=pl.ANY)] + [vmem] * 7,
-        out_specs=vmem,
+        in_specs=[vmem, hbm] + [vmem] * 7,
+        out_specs=hbm,
         scratch_shapes=[
             pltpu.VMEM((4 * npc, 4 * npc), bf16),
             pltpu.VMEM((cells // GROUP, GROUP * npc, 256), bf16),
             pltpu.VMEM((256, rim), bf16),
             pltpu.VMEM((256, rim), bf16),
+            pltpu.VMEM((cells // 2, 2 * npc), jnp.int32),
+            pltpu.VMEM((cells // 2, 2 * npc), f32),
+            pltpu.VMEM((128, 128), jnp.int32),
+            pltpu.VMEM((128, 128), f32),
             pltpu.VMEM((2, rows, ext_len), f32),
             pltpu.VMEM((2, rows, ext_len), f32),
             pltpu.VMEM((2, rows, rim), f32),
@@ -355,13 +432,21 @@
             pltpu.VMEM((2, rows, rim), f32),
             pltpu.VMEM((2, rows, rim), f32),
             pltpu.VMEM((rows, nodes), f32),
-            pltpu.VMEM((panel, nodes), f32),
-            pltpu.SemaphoreType.DMA((3,)),
+            pltpu.VMEM((rest, nodes), f32),
+            pltpu.VMEM((rest, nodes), f32),
+            pltpu.VMEM((rows, nodes), f32),
+            pltpu.VMEM((rows, nodes), f32),
+            pltpu.VMEM((half, nodes), f32),
+            pltpu.SemaphoreType.DMA,
+            pltpu.SemaphoreType.DMA((2,)),
+            pltpu.SemaphoreType.DMA((2,)),
             pltpu.SemaphoreType.DMA((2, 2)),
             pltpu.SemaphoreType.DMA((2, 2)),
             pltpu.SemaphoreType.DMA((2, 2)),
             pltpu.SemaphoreType.DMA((2, 2)),
-            pltpu.SemaphoreType.DMA((2,)),
+            pltpu.SemaphoreType.DMA((parts,)),
+            pltpu.SemaphoreType.DMA((parts,)),
+            pltpu.SemaphoreType.DMA((parts,)),
         ],
         compiler_params=pltpu.CompilerParams(
             collective_id=0, has_side_effects=True, vmem_limit_bytes=52 * 2**20
@@ -371,8 +456,8 @@
         orbitals,
         others,
         potential.reshape(1, nodes),
-        index,
-        scale,
+        connectivity,
+        cell_scale.reshape(cells // 128, 128),
         send_up.reshape(rim // 128, 128),
         send_down.reshape(rim // 128, 128),
         stiffness,

time: 68.4 us -> 70.8 us (1.035); the launches traced: 68.2 us -> 69.8 us
  local copies, waits for them, and re-layouts: 5.34 us -> 9.79 us
  Pallas kernels: 62.8 us -> 59.9 us
    unnamed x19, local copies, waits for them, and re-layouts: 4.66 us -> 9.79 us
    pallas_call x1, Pallas kernels: 62.8 us -> 59.9 us  [body(): pl.pallas_call(functools.partial(kernel, lax.axis_size('domain')), out_sh...]
where the time goes in v2:
time: 70.8 us; the launch traced here: 69.8 us
  Pallas kernels  59.9 us (85%)
  local copies, waits for them, and re-layouts  9.79 us (14%)
    pallas_call x1, Pallas kernels, body(): pl.pallas_call(functools.partial(kernel, lax.axis_size('domain')), out_sh...  59.9 us
    unnamed x19, local copies, waits for them, and re-layouts  9.79 us

profile of v2, /device:TPU:193, one launch (start us, length us, event | category | flops | bytes accessed | tf_op | source)
XLA Modules:
  0.0 69.8 jit_solution(18320315379851290196)
XLA Ops:
  0.0 0.0 copy-start.8
  0.0 0.7 copy-done.8
  0.7 0.0 copy-start
  0.7 1.1 %copy-done = f32[96,2048]{1,0:T(8,128)S(1)} copy-done((f32[96,2048]{1,0:T(8,128)S(1)}, f32[96,2048]{1,0:T(8,128)}, u32[]{:S(2)}) %copy-start) | copy-done | bytes 786456
  1.8 0.0 copy-start.1
  1.8 0.9 %copy-done.1 = f32[32,2048]{1,0:T(8,128)S(1)} copy-done((f32[32,2048]{1,0:T(8,128)S(1)}, f32[32,2048]{1,0:T(8,128)}, u32[]{:S(2)}) %copy-start.1) | copy-done | bytes 262168
  2.8 0.0 copy-start.2
  2.8 0.9 %copy-done.2 = f32[256,256]{1,0:T(8,128)S(1)} copy-done((f32[256,256]{1,0:T(8,128)S(1)}, f32[256,256]{1,0:T(8,128)}, u32[]{:S(2)}) %copy-start.2) | copy-done | bytes 262168
  3.7 0.0 copy-start.3
  3.7 0.9 %copy-done.3 = s32[64,768]{1,0:T(8,128)S(1)} copy-done((s32[64,768]{1,0:T(8,128)S(1)}, s32[64,768]{1,0:T(8,128)}, u32[]{:S(2)}) %copy-start.3) | copy-done | bytes 196632
  4.7 0.0 copy-start.4
  4.7 0.8 %copy-done.4 = f32[64,64]{1,0:T(8,128)S(1)} copy-done((f32[64,64]{1,0:T(8,128)S(1)}, f32[64,64]{1,0:T(8,128)}, u32[]{:S(2)}) %copy-start.4) | copy-done | bytes 16408
  5.4 0.0 copy-start.5
  5.4 0.7 copy-done.5
  6.1 0.0 copy-start.6
  6.1 0.7 copy-done.6
  6.8 0.0 copy-start.7
  6.8 0.7 copy-done.7
  7.5 59.9 %filter_rotate.1 = f32[128,2048]{1,0:T(8,128)} custom-call(f32[32,2048]{1,0:T(8,128)S(1)} %copy-done.1, f32[96,2048]{1,0:T(8,128)S(1)} %copy-done, f32[1,2048]{1,0:T(1,128)S(1)} %bitcast.4, s32[64,768]{1,0:T(8,128)S(1)} %copy-done.3, f32[6,128]{1,0:T(8,128)S(1)} %bitcast.7, s32[12,128]{1,0:T(8,128)S(1)} %bitcast.5, s32[12,128]{1,0:T(8,128)S(1)} %bitcast.6, ...), custom_call_target="tpu_custom_call" | custom-call | tf_op jit(solution)/shard_map/filter_rotate/pallas_call | solution.py:414
  67.5 2.3 %copy.11 = f32[128,2048]{1,0:T(8,128)} copy(f32[128,2048]{1,0:T(8,128)} %filter_rotate.1) | data formatting | bytes 2097152
Async XLA Ops:
  0.0 0.7 copy-start.8
  0.7 1.1 %copy-start = (f32[96,2048]{1,0:T(8,128)S(1)}, f32[96,2048]{1,0:T(8,128)}, u32[]{:S(2)}) copy-start(f32[96,2048]{1,0:T(8,128)} %others.1) | copy-start | bytes 2359300
  1.8 0.9 %copy-start.1 = (f32[32,2048]{1,0:T(8,128)S(1)}, f32[32,2048]{1,0:T(8,128)}, u32[]{:S(2)}) copy-start(f32[32,2048]{1,0:T(8,128)} %orbitals.1) | copy-start | bytes 786436
  2.8 0.9 %copy-start.2 = (f32[256,256]{1,0:T(8,128)S(1)}, f32[256,256]{1,0:T(8,128)}, u32[]{:S(2)}) copy-start(f32[256,256]{1,0:T(8,128)} %rotation.1) | copy-start | bytes 786436
  3.7 0.9 %copy-start.3 = (s32[64,768]{1,0:T(8,128)S(1)}, s32[64,768]{1,0:T(8,128)}, u32[]{:S(2)}) copy-start(s32[64,768]{1,0:T(8,128)} %connectivity.1) | copy-start | bytes 589828
  4.7 0.8 %copy-start.4 = (f32[64,64]{1,0:T(8,128)S(1)}, f32[64,64]{1,0:T(8,128)}, u32[]{:S(2)}) copy-start(f32[64,64]{1,0:T(8,128)} %stiffness.1) | copy-start | bytes 49156
  5.4 0.7 copy-start.5
  6.1 0.7 copy-start.6
  6.8 0.7 copy-start.7

commit v3 on v2

--- a/solution.py
+++ b/solution.py
@@ -59,16 +59,15 @@
     entries = source.shape[1]
     columns = []
     for j in range(entries // 128):
-        values = source[:, 128 * j : 128 * j + 128]
-        high = values.astype(bf16).astype(f32)
-        low = values - high
-        block = jnp.broadcast_to(list_ref[j : j + 1, :] >> 8, (rows, 128))
-        zero = jnp.zeros_like(values)
+        high, low = split(source[:, 128 * j : 128 * j + 128])
+        block = (list_ref[j : j + 1, :] >> 8).astype(f32).astype(bf16)
+        block = jnp.broadcast_to(block, (rows, 128))
+        zero = jnp.zeros_like(high)
         masks = [block == k for k in range(blocks)]
         columns.append(
             jnp.concatenate(
                 [jnp.where(m, high, zero) for m in masks] + [jnp.where(m, low, zero) for m in masks], axis=0
-            ).astype(bf16)
+            )
         )
     left = jnp.concatenate(columns, axis=1)
     both = lax.dot_general(left, one_hot[...], (((1,), (1,)), ((), ())), preferred_element_type=f32)
@@ -88,21 +87,25 @@
     def step(g, carry):
         base = group_base(g, cells, ext_len)
         local = (index_ref[pl.ds(pl.multiple_of(PAIRS * g, PAIRS), PAIRS), :] - base) & 255
-        lanes = lax.broadcasted_iota(jnp.int32, (256, 128), 0)
+        local = local.astype(f32).astype(bf16)
+        lanes = lax.broadcasted_iota(jnp.int32, (128, 256), 1).astype(f32).astype(bf16)
+        one, zero = jnp.ones((128, 256), bf16), jnp.zeros((128, 256), bf16)
         for h in range(PAIRS):
-            entry = jnp.broadcast_to(local[h : h + 1, :], (256, 128))
-            one_hot[g, 128 * h : 128 * h + 128, :] = jnp.where(lanes == entry, 1.0, 0.0).astype(bf16).T
+            entry = jnp.broadcast_to(local[h : h + 1, :], (128, 128)).T
+            entry = jnp.concatenate([entry, entry], axis=1)
+            one_hot[g, 128 * h : 128 * h + 128, :] = jnp.where(lanes == entry, one, zero)
         return carry
 
-    lax.fori_loop(0, cells // GROUP, step, 0, unroll=2)
-
-
-def run_cells(first, last, unroll, extended, index_ref, scale_ref, pair_stiffness, one_hot, summed):
+    lax.fori_loop(0, cells // GROUP, step, 0, unroll=4)
+
+
+def run_cells(first, count, sign, unroll, extended, index_ref, scale_ref, pair_stiffness, one_hot, summed):
     rows, ext_len = extended.shape
     cells = 2 * index_ref.shape[0]
     row_tiles = rows // 8
 
-    def step(g, carry):
+    def step(i, carry):
+        g = first + sign * i
         base = group_base(g, cells, ext_len)
         source = [
             [extended[8 * o : 8 * o + 8, pl.ds(base + 128 * k, 128)] for k in range(4)] for o in range(row_tiles)
@@ -148,7 +151,7 @@
         summed[:, pl.ds(base + 256, 256)] += added[rows:]
         return carry
 
-    lax.fori_loop(first, last, step, 0, unroll=unroll)
+    lax.fori_loop(0, count, step, 0, unroll=unroll)
 
 
 def pair_rows(block, turn, target):
@@ -168,8 +171,17 @@
 
 def kernel(
     n_domain,
+    hbm_orbitals,
+    others,
+    hbm_potential,
+    hbm_connectivity,
+    hbm_cell_scale,
+    hbm_up_list,
+    hbm_down_list,
+    hbm_stiffness,
+    hbm_rotation,
+    out,
     orbitals,
-    others,
     potential,
     connectivity,
     cell_scale,
@@ -177,7 +189,6 @@
     down_list,
     stiffness,
     rotation,
-    out,
     pair_stiffness,
     one_hot,
     up_hot,
@@ -208,6 +219,7 @@
     filt_send,
     filt_recv,
     out_sems,
+    in_sems,
 ):
     rows, nodes = orbitals.shape
     rim = up_out.shape[2]
@@ -216,6 +228,9 @@
     groups = cells // GROUP
     low_end = 288 // GROUP
     high_start = groups - low_end
+    low_half, high_half = low_end // 2, groups - low_end // 2
+    low_cut = GROUP * low_half * (ext_len - WINDOW) // (cells - 1) // 128 * 128
+    high_cut = GROUP * (high_half - 1) * (ext_len - WINDOW) // (cells - 1) // 128 * 128 + SPAN
     rest = others.shape[0]
     half = out.shape[0]
     piece = nodes // filt_send.shape[0]
@@ -229,9 +244,27 @@
     for target in ({"domain": above}, {"domain": below}, {"band": mate}):
         pl.semaphore_signal(barrier, inc=1, device_id=target, device_id_type=MESH)
 
+    loads = []
+    for k, (source, target) in enumerate(
+        (
+            (hbm_up_list, up_list),
+            (hbm_orbitals, orbitals),
+            (hbm_down_list, down_list),
+            (hbm_connectivity, connectivity),
+            (hbm_cell_scale, cell_scale),
+            (hbm_stiffness, stiffness),
+            (hbm_potential, potential),
+            (hbm_rotation, rotation),
+        )
+    ):
+        loads.append(pltpu.make_async_copy(source, target, in_sems.at[k]))
+        loads[k].start()
     own_copy = pltpu.make_async_copy(others, own_others, own_sem)
     own_copy.start()
+    loads[0].wait()
     list_one_hot(up_list, up_hot)
+    loads[1].wait()
+    loads[2].wait()
     list_one_hot(down_list, down_hot)
 
     def send_ghosts(source, step):
@@ -261,17 +294,33 @@
         sums[step] = jnp.zeros((rows, ext_len), f32)
         return up, down
 
-    def send_back(step, lower):
+    def send_back(step, lower, part):
+        edge = low_cut if lower else high_cut - rim - nodes
+        first = 0 if (part == 0) == lower else edge
+        count = edge if (part == 0) == lower else rim - edge
+        sem = part if lower else 2 + part
         copy = pltpu.make_async_remote_copy(
-            src_ref=sums.at[step, :, pl.ds(0 if lower else rim + nodes, rim)],
-            dst_ref=(up_back if lower else down_back).at[step],
-            send_sem=back_send.at[step, 0 if lower else 1],
-            recv_sem=back_recv.at[step, 0 if lower else 1],
+            src_ref=sums.at[step, :, pl.ds(first if lower else rim + nodes + first, count)],
+            dst_ref=(up_back if lower else down_back).at[step, :, pl.ds(first, count)],
+            send_sem=back_send.at[step, sem],
+            recv_sem=back_recv.at[step, sem],
             device_id={"domain": below if lower else above},
             device_id_type=MESH,
         )
         copy.start()
         return copy
+
+    def lower_cells(step):
+        cells_from(step, 0, low_half, 1, 9)
+        first = send_back(step, True, 0)
+        cells_from(step, low_half, low_end - low_half, 1, 9)
+        return first, send_back(step, True, 1)
+
+    def upper_cells(step):
+        cells_from(step, groups - 1, groups - high_half, -1, 9)
+        first = send_back(step, False, 0)
+        cells_from(step, high_half - 1, high_half - high_start, -1, 9)
+        return first, send_back(step, False, 1)
 
     def send_others(step):
         cut = pl.ds(0, rest // 3 * 2) if step == 0 else pl.ds(rest // 3 * 2, rest // 3)
@@ -286,10 +335,11 @@
         copy.start()
         return copy
 
-    def cells_from(step, first, last, unroll):
+    def cells_from(step, first, count, sign, unroll):
         run_cells(
             first,
-            last,
+            count,
+            sign,
             unroll,
             extended.at[step],
             index_ref,
@@ -300,6 +350,8 @@
         )
 
     up, down = send_ghosts(orbitals, 0)
+    for load in loads[3:]:
+        load.wait()
     build_stiffness(stiffness, pair_stiffness)
     for k in range(cells // 128):
         cut = slice(128 * k, 128 * k + 128)
@@ -310,17 +362,17 @@
     build_cells(index_ref, one_hot, cells, ext_len)
     own_copy.wait()
     up.wait()
+    down.wait()
     others_0 = send_others(0)
-    cells_from(0, 0, low_end, 9)
-    lower = send_back(0, True)
-    down.wait()
-    cells_from(0, high_start, groups, 9)
-    upper = send_back(0, False)
-    cells_from(0, low_end, high_start, 6)
+    lower = lower_cells(0)
+    upper = upper_cells(0)
+    cells_from(0, low_end, high_start - low_end, 1, 6)
     current[...] = sums[0, :, rim : rim + nodes]
-    lower.wait()
+    for copy in lower:
+        copy.wait()
     place(up_back.at[0], up_list, up_hot, current)
-    upper.wait()
+    for copy in upper:
+        copy.wait()
     place(down_back.at[0], down_list, down_hot, current)
     for k in range(nodes // 256):
         cut = slice(256 * k, 256 * k + 256)
@@ -328,14 +380,12 @@
         current[:, cut] = (current[:, cut] + potential[:, cut] * before - CENTER * before) * (1.0 / HALF)
 
     up, down = send_ghosts(current, 1)
-    cells_from(1, low_end, high_start, 6)
+    cells_from(1, low_end, high_start - low_end, 1, 6)
     up.wait()
+    lower = lower_cells(1)
+    down.wait()
     others_1 = send_others(1)
-    cells_from(1, 0, low_end, 9)
-    lower = send_back(1, True)
-    down.wait()
-    cells_from(1, high_start, groups, 9)
-    upper = send_back(1, False)
+    upper = upper_cells(1)
     own_filt[...] = sums[1, :, rim : rim + nodes]
 
     columns = pl.ds(pl.multiple_of(band * half, 128), half)
@@ -361,9 +411,11 @@
     own_weights = pieces(weights_of(rows * band, rows))
     mate_weights = pieces(weights_of(rows * mate, rows))
 
-    lower.wait()
+    for copy in lower:
+        copy.wait()
     place(up_back.at[1], up_list, up_hot, own_filt)
-    upper.wait()
+    for copy in upper:
+        copy.wait()
     place(down_back.at[1], down_list, down_hot, own_filt)
     copies = []
     for k in range(nodes // piece):
@@ -409,14 +461,21 @@
     panel = rotation.shape[0]
     half = panel // lax.axis_size("band")
     parts = 4
-    vmem = pl.BlockSpec(memory_space=pltpu.VMEM)
     hbm = pl.BlockSpec(memory_space=pl.ANY)
     return pl.pallas_call(
         functools.partial(kernel, lax.axis_size("domain")),
         out_shape=jax.ShapeDtypeStruct((half, nodes), f32),
-        in_specs=[vmem, hbm] + [vmem] * 7,
+        in_specs=[hbm] * 9,
         out_specs=hbm,
         scratch_shapes=[
+            pltpu.VMEM((rows, nodes), f32),
+            pltpu.VMEM((1, nodes), f32),
+            pltpu.VMEM((npc, cells), jnp.int32),
+            pltpu.VMEM((cells // 128, 128), f32),
+            pltpu.VMEM((rim // 128, 128), jnp.int32),
+            pltpu.VMEM((rim // 128, 128), jnp.int32),
+            pltpu.VMEM((npc, npc), f32),
+            pltpu.VMEM((panel, panel), f32),
             pltpu.VMEM((4 * npc, 4 * npc), bf16),
             pltpu.VMEM((cells // GROUP, GROUP * npc, 256), bf16),
             pltpu.VMEM((256, rim), bf16),
@@ -442,14 +501,15 @@
             pltpu.SemaphoreType.DMA((2,)),
             pltpu.SemaphoreType.DMA((2, 2)),
             pltpu.SemaphoreType.DMA((2, 2)),
-            pltpu.SemaphoreType.DMA((2, 2)),
-            pltpu.SemaphoreType.DMA((2, 2)),
+            pltpu.SemaphoreType.DMA((2, 4)),
+            pltpu.SemaphoreType.DMA((2, 4)),
             pltpu.SemaphoreType.DMA((parts,)),
             pltpu.SemaphoreType.DMA((parts,)),
             pltpu.SemaphoreType.DMA((parts,)),
+            pltpu.SemaphoreType.DMA((8,)),
         ],
         compiler_params=pltpu.CompilerParams(
-            collective_id=0, has_side_effects=True, vmem_limit_bytes=52 * 2**20
+            collective_id=0, has_side_effects=True, vmem_limit_bytes=64 * 2**20
         ),
         name="filter_rotate",
     )(

time: 70.8 us -> 62 us (0.88)
  the two profiles are of different devices: /device:TPU:193 before, /device:TPU:1 now
where the time goes in v3:
time: 62 us; the launch traced here: 61.9 us
  Pallas kernels  59.6 us (96%)
  local copies, waits for them, and re-layouts  2.3 us (4%)
    pallas_call x1, Pallas kernels, body(): pl.pallas_call(functools.partial(kernel, lax.axis_size('domain')), out_sh...  59.6 us
    unnamed x1, local copies, waits for them, and re-layouts  2.3 us

profile of v3, /device:TPU:1, one launch (start us, length us, event | category | flops | bytes accessed | tf_op | source)
XLA Modules:
  0.0 61.9 jit_solution(7105122385111695250)
XLA Ops:
  0.0 59.6 %filter_rotate.1 = f32[128,2048]{1,0:T(8,128)} custom-call(f32[32,2048]{1,0:T(8,128)} %hbm_orbitals.1, f32[96,2048]{1,0:T(8,128)} %others.1, f32[1,2048]{1,0:T(1,128)} %bitcast.4, s32[64,768]{1,0:T(8,128)} %hbm_connectivity.1, f32[6,128]{1,0:T(8,128)} %bitcast.7, s32[12,128]{1,0:T(8,128)} %bitcast.5, s32[12,128]{1,0:T(8,128)} %bitcast.6, ...), custom_call_target="tpu_custom_call" | custom-call | tf_op jit(solution)/shard_map/filter_rotate/pallas_call | solution.py:465
  59.6 2.3 %copy.11 = f32[128,2048]{1,0:T(8,128)} copy(f32[128,2048]{1,0:T(8,128)} %filter_rotate.1) | data formatting | bytes 2097152

commit v4 on v3

--- a/solution.py
+++ b/solution.py
@@ -323,7 +323,8 @@
         return first, send_back(step, False, 1)
 
     def send_others(step):
-        cut = pl.ds(0, rest // 3 * 2) if step == 0 else pl.ds(rest // 3 * 2, rest // 3)
+        edges = (0, rest // 12 * 7, rest // 4 * 3, rest)
+        cut = pl.ds(edges[step], edges[step + 1] - edges[step])
         copy = pltpu.make_async_remote_copy(
             src_ref=own_others.at[cut, :],
             dst_ref=mate_others.at[cut, :],
@@ -373,6 +374,7 @@
     place(up_back.at[0], up_list, up_hot, current)
     for copy in upper:
         copy.wait()
+    others_1 = send_others(1)
     place(down_back.at[0], down_list, down_hot, current)
     for k in range(nodes // 256):
         cut = slice(256 * k, 256 * k + 256)
@@ -382,9 +384,9 @@
     up, down = send_ghosts(current, 1)
     cells_from(1, low_end, high_start - low_end, 1, 6)
     up.wait()
+    others_2 = send_others(2)
     lower = lower_cells(1)
     down.wait()
-    others_1 = send_others(1)
     upper = upper_cells(1)
     own_filt[...] = sums[1, :, rim : rim + nodes]
 
@@ -395,6 +397,7 @@
 
     others_0.wait()
     others_1.wait()
+    others_2.wait()
     high, low = split(
         jnp.concatenate([weights_of(2 * rows + rest * band, rest), weights_of(2 * rows + rest * mate, rest)], axis=1)
     )
@@ -497,8 +500,8 @@
             pltpu.VMEM((rows, nodes), f32),
             pltpu.VMEM((half, nodes), f32),
             pltpu.SemaphoreType.DMA,
-            pltpu.SemaphoreType.DMA((2,)),
-            pltpu.SemaphoreType.DMA((2,)),
+            pltpu.SemaphoreType.DMA((3,)),
+            pltpu.SemaphoreType.DMA((3,)),
             pltpu.SemaphoreType.DMA((2, 2)),
             pltpu.SemaphoreType.DMA((2, 2)),
             pltpu.SemaphoreType.DMA((2, 4)),

time: 62 us -> 59.1 us (0.953)
  the two profiles are of different devices: /device:TPU:1 before, /device:TPU:193 now
where the time goes in v4:
time: 59.1 us; the launch traced here: 58.2 us
  Pallas kernels  55.9 us (95%)
  local copies, waits for them, and re-layouts  2.3 us (4%)
    pallas_call x1, Pallas kernels, body(): pl.pallas_call(functools.partial(kernel, lax.axis_size('domain')), out_sh...  55.9 us
    unnamed x1, local copies, waits for them, and re-layouts  2.3 us

profile of v4, /device:TPU:193, one launch (start us, length us, event | category | flops | bytes accessed | tf_op | source)
XLA Modules:
  0.0 58.2 jit_solution(11248587683843333040)
XLA Ops:
  0.0 55.9 %filter_rotate.1 = f32[128,2048]{1,0:T(8,128)} custom-call(f32[32,2048]{1,0:T(8,128)} %hbm_orbitals.1, f32[96,2048]{1,0:T(8,128)} %others.1, f32[1,2048]{1,0:T(1,128)} %bitcast.4, s32[64,768]{1,0:T(8,128)} %hbm_connectivity.1, f32[6,128]{1,0:T(8,128)} %bitcast.7, s32[12,128]{1,0:T(8,128)} %bitcast.5, s32[12,128]{1,0:T(8,128)} %bitcast.6, ...), custom_call_target="tpu_custom_call" | custom-call | tf_op jit(solution)/shard_map/filter_rotate/pallas_call | solution.py:468
  55.9 2.3 %copy.11 = f32[128,2048]{1,0:T(8,128)} copy(f32[128,2048]{1,0:T(8,128)} %filter_rotate.1) | data formatting | bytes 2097152

commit v5 on v4

--- a/solution.py
+++ b/solution.py
@@ -180,7 +180,8 @@
     hbm_down_list,
     hbm_stiffness,
     hbm_rotation,
-    out,
+    out_top,
+    out_rest,
     orbitals,
     potential,
     connectivity,
@@ -232,7 +233,8 @@
     low_cut = GROUP * low_half * (ext_len - WINDOW) // (cells - 1) // 128 * 128
     high_cut = GROUP * (high_half - 1) * (ext_len - WINDOW) // (cells - 1) // 128 * 128 + SPAN
     rest = others.shape[0]
-    half = out.shape[0]
+    top = out_top.shape[0]
+    half = top + out_rest.shape[0]
     piece = nodes // filt_send.shape[0]
 
     me = lax.axis_index("domain")
@@ -444,11 +446,11 @@
         for j in range(piece // 256):
             cut = slice(piece * k + 256 * j, piece * k + 256 * j + 256)
             rotated[:, cut] += times(mate_weights, mate_filt[:, cut])
-        write = pltpu.make_async_copy(
-            rotated.at[:, pl.ds(piece * k, piece)], out.at[:, pl.ds(piece * k, piece)], out_sems.at[k]
-        )
-        write.start()
-        writes.append(write)
+        cut = pl.ds(piece * k, piece)
+        for j, (target, first, count) in enumerate(((out_top, 0, top), (out_rest, top, half - top))):
+            write = pltpu.make_async_copy(rotated.at[pl.ds(first, count), cut], target.at[:, cut], out_sems.at[j, k])
+            write.start()
+            writes.append(write)
     for write in writes:
         write.wait()
 
@@ -465,11 +467,11 @@
     half = panel // lax.axis_size("band")
     parts = 4
     hbm = pl.BlockSpec(memory_space=pl.ANY)
-    return pl.pallas_call(
+    halves = pl.pallas_call(
         functools.partial(kernel, lax.axis_size("domain")),
-        out_shape=jax.ShapeDtypeStruct((half, nodes), f32),
+        out_shape=[jax.ShapeDtypeStruct((half // 2, nodes), f32)] * 2,
         in_specs=[hbm] * 9,
-        out_specs=hbm,
+        out_specs=[hbm] * 2,
         scratch_shapes=[
             pltpu.VMEM((rows, nodes), f32),
             pltpu.VMEM((1, nodes), f32),
@@ -508,7 +510,7 @@
             pltpu.SemaphoreType.DMA((2, 4)),
             pltpu.SemaphoreType.DMA((parts,)),
             pltpu.SemaphoreType.DMA((parts,)),
-            pltpu.SemaphoreType.DMA((parts,)),
+            pltpu.SemaphoreType.DMA((2, parts)),
             pltpu.SemaphoreType.DMA((8,)),
         ],
         compiler_params=pltpu.CompilerParams(
@@ -526,6 +528,7 @@
         stiffness,
         rotation,
     )
+    return jnp.concatenate(halves, axis=0)
 
 
 def solution(mesh):

time: 59.1 us -> 59.1 us (level)
  local copies, waits for them, and re-layouts: 2.3 us -> 0 us
  other arithmetic: 0 us -> 2.27 us
    unnamed x1 -> x0, local copies, waits for them, and re-layouts: 2.3 us -> none
    concatenate x0 -> x1, other arithmetic: none -> 2.27 us  [body(): return jnp.concatenate(halves, axis=0)]
where the time goes in v5:
time: 59.1 us; the launch traced here: 58.2 us
  Pallas kernels  55.9 us (95%)
  other arithmetic  2.27 us (4%)
    pallas_call x1, Pallas kernels, body(): pl.pallas_call(functools.partial(kernel, lax.axis_size('domain')), out_sh...  55.9 us
    concatenate x1, other arithmetic, body(): return jnp.concatenate(halves, axis=0)  2.27 us

profile of v5, /device:TPU:193, one launch (start us, length us, event | category | flops | bytes accessed | tf_op | source)
XLA Modules:
  0.0 58.2 jit_solution(3914552108817919983)
XLA Ops:
  0.0 55.9 %filter_rotate.1 = (f32[64,2048]{1,0:T(8,128)}, f32[64,2048]{1,0:T(8,128)}) custom-call(f32[32,2048]{1,0:T(8,128)} %hbm_orbitals.1, f32[96,2048]{1,0:T(8,128)} %others.1, f32[1,2048]{1,0:T(1,128)} %bitcast.4, s32[64,768]{1,0:T(8,128)} %hbm_connectivity.1, f32[6,128]{1,0:T(8,128)} %bitcast.7, s32[12,128]{1,0:T(8,128)} %bitcast.5, s32[12,128]{1,0:T(8,128)} %bitcast.6, ...), custom_call_target="tpu_custom_call" | custom-call | tf_op jit(solution)/shard_map/filter_rotate/pallas_call | solution.py:470
  55.9 2.3 %pad_maximum_fusion = f32[128,2048]{1,0:T(8,128)} fusion(f32[64,2048]{1,0:T(8,128)} %get-tuple-element.8, f32[64,2048]{1,0:T(8,128)} %get-tuple-element.7), kind=kLoop, calls=%fused_computation | loop fusion | flops 262144 | bytes 2097152 | tf_op jit(solution)/shard_map/concatenate | solution.py:531
